TPU v7x, 32 devices: a whole 2x2x4 slice. The times are simulated.
32 devices in a mesh: seq: 8 (over y, x, core), head: 4 (over z).
Axes of the slice: x: 2, y: 2, z: 4, core: 2. Of those that a mesh axis runs over, the one named last changes fastest.
Arguments:
- queries: bfloat16 [512, 8192], P('seq', 'head'), may hold values from -6 to 6
- keys: bfloat16 [512, 1024], P('seq'), may hold values from -6 to 6
- values: bfloat16 [512, 1024], P('seq'), may hold values from -6 to 6
- vertical: int32 [64, 8], replicated, may hold values from -1 to 7, as said below
- slash: int32 [64, 8], replicated, may hold values from -1 to 7, as said below
- plan: int32 [64], replicated, may hold values from 0 to 63, each once
Outputs:
- attended: bfloat16 [512, 8192], P('seq', 'head')
Inputs may be any that keep to these rules, and one draw needn't show every extreme that they name: `vertical`: entries of 0 or more name key blocks of 64 positions; -1 marks an unused entry, and every row has at least one used entry. `slash`: entries of 0 or more are offsets back from a query's own block; -1 marks an unused entry; the first entry of every row is 0. `plan`: A permutation of the query heads.
All inputs are finite; a program needn't handle non-finite values.
Results may differ from a plain program's by a relative error of at most 0.0044.
Values may be sent and summed in bfloat16 or wider, within the bound.
No kernel may reach another device: no remote copies, remote signals or barrier semaphores. Data moves between devices by JAX's collectives and lax.ppermute only.
A program may use at most 64 MiB of HBM per device.

v0:
```python
import functools
import math

import jax
import jax.numpy as jnp
from jax import lax
from jax.experimental import pallas as pl
from jax.experimental.pallas import tpu as pltpu
from jax.sharding import PartitionSpec as P

HD = 128
QH = 64
KVH = 8
BLK = 64
GROUP = QH // KVH
HEADS_AT_ONCE = 4
LANES = 128

floor_value = -1e30

SMEM = pl.BlockSpec(memory_space=pltpu.SMEM)
VMEM = pl.BlockSpec(memory_space=pltpu.VMEM)
ANY = pl.BlockSpec(memory_space=pl.ANY)
SMALL = 1024 * 1024


def shift_of(size):
    assert size & (size - 1) == 0
    return size.bit_length() - 1


def entry_bits(table):
    bits = jnp.zeros((1, table.shape[1]), jnp.int32)
    for entry in range(table.shape[0]):
        named = table[entry : entry + 1, :]
        bits = bits | jnp.where(named >= 0, jnp.int32(1) << jnp.maximum(named, 0), 0)
    return bits


class Tally:
    def __init__(self, head_size, held):
        self.width = shift_of(held) + 1
        self.per_word = 31 // self.width
        self.words = [jnp.int32(0)] * -(-head_size // self.per_word)

    def rank_and_count(self, owner):
        if len(self.words) == 1:
            at = owner * self.width
            rank = self.words[0] >> at
            self.words[0] = self.words[0] + (jnp.int32(1) << at)
        else:
            word = owner // self.per_word
            at = (owner - word * self.per_word) * self.width
            held_word = self.words[0]
            for index in range(1, len(self.words)):
                held_word = jnp.where(word == index, self.words[index], held_word)
            rank = held_word >> at
            one = jnp.int32(1) << at
            self.words = [w + jnp.where(word == index, one, 0) for index, w in enumerate(self.words)]
        return rank & ((1 << self.width) - 1)

    def count(self, owner):
        word = self.words[owner // self.per_word]
        return (word >> (owner % self.per_word * self.width)) & ((1 << self.width) - 1)


def route_kernel(head_size, held, levels, plan, vertical, slash, send, slots, level, bits):
    own = lax.axis_index("head")
    most = [jnp.int32(0)] * head_size
    for target in range(head_size):
        tally = Tally(head_size, held)
        for t in range(held):
            head = plan[target * held + t]
            owner = head >> shift_of(held)
            rank = tally.rank_and_count(owner)
            send[jnp.where(owner == own, head & (held - 1), held)] = ((owner ^ target) << shift_of(held)) + rank
        for owner in range(head_size):
            most[owner ^ target] = jnp.maximum(most[owner ^ target], tally.count(owner))
    tally = Tally(head_size, held)
    for distance in range(head_size):
        slots[head_size * held + distance] = 0
    for t in range(held):
        owner = plan[own * held + t] >> shift_of(held)
        rank = tally.rank_and_count(owner)
        distance = owner ^ own
        slots[(distance << shift_of(held)) + rank] = t
        slots[head_size * held + distance] = rank + 1
    chosen = jnp.int32(len(levels) - 1)
    for index in reversed(range(len(levels) - 1)):
        fits = most[1] <= levels[index][1]
        for distance in range(2, head_size):
            fits = fits & (most[distance] <= levels[index][distance])
        chosen = jnp.where(fits, index, chosen)
    level[0] = chosen
    bits[0:1, :] = entry_bits(vertical)
    bits[1:2, :] = entry_bits(slash)


def attention_kernel(
    seq_size, held, kv_heads, send, bits, kv_own, kv_other, query_ref, out_ref, send_here, copied
):
    send_copy = pltpu.make_async_copy(send, send_here, copied)
    send_copy.start()
    own_seq = lax.axis_index("seq")
    rest = (send_copy, bits, kv_own, kv_other, query_ref, out_ref, send_here)

    @pl.when(own_seq < 2)
    def _():
        attend(1, held, kv_heads, *rest)

    @pl.when(own_seq >= 2)
    def _():
        attend(seq_size // 2, held, kv_heads, *rest)


def attend(chips, held, kv_heads, send_copy, bits, kv_own, kv_other, query_ref, out_ref, send_here):
    query_len = query_ref.shape[0]
    key_len = query_len
    own_seq = lax.axis_index("seq")
    own_head = lax.axis_index("head")
    half = chips * key_len

    piece = lax.broadcasted_iota(jnp.int32, (1, 2 * half), 1) // key_len
    core = jnp.where(piece < chips, own_seq & 1, 1 - (own_seq & 1))
    block = ((own_seq >> 1) ^ (piece & (chips - 1))) * 2 + core
    back = own_seq - block
    present = back >= 0
    back_shift = jnp.maximum(back, 0)
    heads = own_head * held + lax.broadcasted_iota(jnp.int32, (held, bits.shape[1]), 0)
    is_head = lax.broadcasted_iota(jnp.int32, (held, bits.shape[1]), 1) == heads
    vertical_bits, slash_bits = (
        jnp.sum(jnp.where(is_head, bits[kind : kind + 1, :], 0), axis=1, keepdims=True) for kind in range(2)
    )
    hit = ((vertical_bits >> block) | (slash_bits >> back_shift)) & 1
    bias = jnp.where((hit == 1) & present, 0.0, floor_value)
    row = lax.broadcasted_iota(jnp.int32, (query_len, LANES), 0)
    column = lax.broadcasted_iota(jnp.int32, (query_len, LANES), 1)
    causal = (column <= row) | (column >= key_len)
    score_scale = HD ** (-0.5) * math.log2(math.e)
    per_kv = held // kv_heads

    def scores_of(lead):
        heads = range(lead, min(lead + HEADS_AT_ONCE, held))
        key_at = lead // per_kv * HD
        key = jnp.concatenate([ref[:half, key_at : key_at + HD] for ref in (kv_own, kv_other)], axis=0)
        query = jnp.concatenate([query_ref[:, i * HD : (i + 1) * HD] for i in heads], axis=0)
        return lax.dot_general(
            query, key, (((1,), (1,)), ((), ())), preferred_element_type=jnp.float32
        )

    ready = []
    following = scores_of(0)
    for lead in range(0, held, HEADS_AT_ONCE):
        heads = range(lead, min(lead + HEADS_AT_ONCE, held))
        scores = following
        if lead + HEADS_AT_ONCE < held:
            following = scores_of(lead + HEADS_AT_ONCE)
        value_at = (lead // per_kv + kv_heads) * HD
        value = jnp.concatenate([ref[:half, value_at : value_at + HD] for ref in (kv_own, kv_other)], axis=0)
        weights = []
        totals = []
        for at, i in enumerate(heads):
            masked = scores[at * query_len : (at + 1) * query_len] + bias[i : i + 1, :]
            own_block = jnp.where(causal, masked[:, :LANES], floor_value)
            masked = own_block if 2 * half == LANES else jnp.concatenate([own_block, masked[:, LANES:]], axis=1)
            row_max = jnp.max(masked, axis=1, keepdims=True)
            weight = jnp.exp2((masked - row_max) * score_scale)
            totals.append(1.0 / jnp.sum(weight, axis=1, keepdims=True))
            weights.append(weight.astype(jnp.bfloat16))
        mixture = jnp.dot(
            jnp.concatenate(weights, axis=0), value, preferred_element_type=jnp.float32
        )
        for at, i in enumerate(heads):
            mix = mixture[at * query_len : (at + 1) * query_len]
            ready.append((i, (mix * totals[at]).astype(out_ref.dtype)))
        if chips > 1 or lead + HEADS_AT_ONCE >= held:
            if chips == 1 or lead == 0:
                send_copy.wait()
            for i, rows in ready:
                out_ref[send_here[i]] = rows
            ready = []


def place_kernel(head_size, held, sources, slots, *refs):
    out_ref, done = refs[-2:]
    for (distance, capacity), ref in zip(sources, refs):
        arriving = slots[head_size * held + distance]
        for rank in range(capacity):

            @pl.when(rank < arriving)
            def _(ref=ref, rank=rank, distance=distance):
                at = pl.multiple_of(slots[distance * held + rank] * HD, HD)
                pltpu.make_async_copy(ref.at[rank], out_ref.at[:, pl.ds(at, HD)], done).start()

    pltpu.make_async_copy(out_ref, out_ref, done).wait()


SHAPES = (
    (4, 5, 4), (7, 4, 4), (4, 6, 4), (5, 5, 5), (8, 5, 4), (4, 4, 6), (4, 7, 4), (5, 6, 5), (6, 4, 6), (6, 6, 4),
    (8, 5, 5), (9, 6, 4), (4, 4, 7), (5, 5, 6), (5, 7, 5), (6, 6, 6), (7, 4, 7), (8, 7, 4), (9, 6, 5), (5, 5, 7),
    (5, 8, 5), (6, 7, 6), (7, 5, 7), (8, 4, 8), (9, 7, 5), (11, 6, 6), (6, 6, 7), (5, 9, 5), (6, 8, 6), (7, 7, 7),
    (8, 5, 8), (6, 6, 8), (7, 8, 7), (6, 6, 9), (8, 8, 8), (7, 10, 7), (9, 9, 9), (11, 10, 10),
)


def capacity_levels(head_size, held):
    shapes = [tuple(max(1, held * part // 16) for part in shape) for shape in SHAPES]
    levels = []
    for near, *far in shapes + [(held,) * 3]:
        level = tuple(near if m < head_size // 2 else far[m % 2] for m in range(head_size))
        if level not in levels:
            levels.append(level)
    return levels


def exchange(head_size, held, capacities, packed, slots):
    order = sorted(range(1, head_size), key=lambda m: (m >= head_size // 2, -m))
    arrived = [
        lax.ppermute(
            packed[m * held : m * held + capacities[m]], "head", [(i, i ^ m) for i in range(head_size)]
        )
        for m in order
    ]
    return pl.pallas_call(
        functools.partial(place_kernel, head_size, held, [(0, held)] + [(m, capacities[m]) for m in order]),
        out_shape=pltpu.HBM((packed.shape[1], held * HD), packed.dtype),
        in_specs=[SMEM] + [ANY] * head_size,
        out_specs=pl.BlockSpec(memory_space=pltpu.HBM),
        scratch_shapes=[pltpu.SemaphoreType.DMA],
        compiler_params=pltpu.CompilerParams(vmem_limit_bytes=SMALL),
        name="place",
    )(slots, packed, *arrived)


def per_device(queries, keys, values, vertical, slash, plan):
    seq_size = lax.axis_size("seq")
    head_size = lax.axis_size("head")
    query_len = queries.shape[0]
    held = queries.shape[1] // HD
    kv_heads = max(1, held // GROUP)
    chips = seq_size // 2
    assert query_len == BLK and plan.shape[0] == held * head_size and chips & (chips - 1) == 0

    levels = capacity_levels(head_size, held)
    send, slots, level, bits = pl.pallas_call(
        functools.partial(route_kernel, head_size, held, levels),
        out_shape=[
            jax.ShapeDtypeStruct((held + 1,), jnp.int32),
            jax.ShapeDtypeStruct((head_size * held + head_size,), jnp.int32),
            jax.ShapeDtypeStruct((1,), jnp.int32),
            jax.ShapeDtypeStruct((2, vertical.shape[0]), jnp.int32),
        ],
        in_specs=[SMEM, VMEM, VMEM],
        out_specs=[SMEM] * 3 + [VMEM],
        compiler_params=pltpu.CompilerParams(vmem_limit_bytes=SMALL),
        name="route",
    )(plan, vertical.T, slash.T)

    kv_at = lax.axis_index("head") * held // GROUP * HD
    kv = jnp.concatenate(
        [lax.dynamic_slice_in_dim(rows, kv_at, kv_heads * HD, axis=1) for rows in (keys, values)], axis=1
    )
    pieces = [kv]
    for m in range(1, chips):
        pairs = [(i, i ^ (2 * m)) for i in range(seq_size)]
        pieces.append(lax.ppermute(kv, "seq", pairs))
    pieces, send, slots, level, bits = lax.optimization_barrier((pieces, send, slots, level, bits))
    kv_own = jnp.concatenate(pieces, axis=0)
    kv_other = lax.ppermute(kv_own, "seq", [(i, i ^ 1) for i in range(seq_size)])

    packed = pl.pallas_call(
        functools.partial(attention_kernel, seq_size, held, kv_heads),
        out_shape=jax.ShapeDtypeStruct((head_size * held, query_len, HD), jnp.bfloat16),
        in_specs=[ANY] + [VMEM] * 4,
        out_specs=VMEM,
        scratch_shapes=[pltpu.SMEM(send.shape, send.dtype), pltpu.SemaphoreType.DMA],
        compiler_params=pltpu.CompilerParams(vmem_limit_bytes=40 * 1024 * 1024),
        name="attention",
    )(send, bits, kv_own, kv_other, queries)

    return lax.switch(
        level[0],
        [functools.partial(exchange, head_size, held, capacities) for capacities in levels],
        packed,
        slots,
    )


def solution(mesh):
    in_specs = (P("seq", "head"), P("seq", None), P("seq", None), P(), P(), P())
    out_specs = P("seq", "head")
    return jax.shard_map(
        per_device, mesh=mesh, in_specs=in_specs, out_specs=out_specs, check_vma=False
    )
```

profile of v0, /device:TPU:0, one launch (start us, length us, event | category | flops | bytes accessed | tf_op | source)
XLA Modules:
  0.0 24.9 jit_solution(9415129333859854562)
XLA Ops:
  0.0 0.8 %constant_dynamic-slice_fusion = (bf16[64,256]{1,0:T(8,128)(2,1)S(1)}, bf16[64,256]{1,0:T(8,128)(2,1)S(1)}) fusion(bf16[64,1024]{1,0:T(8,128)(2,1)} %param.47, s32[]{:T(128)S(6)} %select_n.10, bf16[64,1024]{1,0:T(8,128)(2,1)} %param.46), kind=kLoop, calls=%fused_computation.5 | loop fusion | bytes 131076 | tf_op jit(solution)/shard_map/dynamic_slice | solution.py:261
  0.8 0.0 copy-start.1
  0.8 0.0 copy-start.2
  0.8 4.0 %collective-permute-start.119 = (bf16[64,512]{1,0:T(8,128)(2,1)S(1)}, bf16[64,512]{1,0:T(8,128)(2,1)S(1)}, u32[]{:S(2)}, u32[]{:S(2)}) collective-permute-start(bf16[64,512]{1,0:T(8,128)(2,1)S(1)} %pad_maximum_fusion), channel_id=1, source_target_pairs={{0,24},{4,28},{8,16},{12,20},{16,8},{20,12},{24,0},{28,4},{1,25},{... | collective-permute-start | bytes 196616 | tf_op jit(solution)/shard_map/ppermute | solution.py:266
  4.8 0.5 %collective-permute-start.118 = (bf16[64,512]{1,0:T(8,128)(2,1)S(1)}, bf16[64,512]{1,0:T(8,128)(2,1)S(1)}, u32[]{:S(2)}, u32[]{:S(2)}) collective-permute-start(bf16[64,512]{1,0:T(8,128)(2,1)S(1)} %pad_maximum_fusion), channel_id=1, source_target_pairs={{0,16},{4,20},{8,24},{12,28},{16,0},{20,4},{24,8},{28,12},{1,17},{... | collective-permute-start | bytes 196616 | tf_op jit(solution)/shard_map/ppermute | solution.py:266
  5.3 0.1 collective-permute-start.117
  5.4 0.0 copy-start.3
  5.4 0.0 copy-done.1
  5.4 0.0 copy-done.2
  5.4 0.6 %copy-done.3 = s32[64]{0:T(128)S(1)} copy-done((s32[64]{0:T(128)S(1)}, s32[64]{0:T(128)}, u32[]{:S(2)}) %copy-start.3) | copy-done | bytes 280
  6.1 1.5 %route.1 = (s32[17]{0:T(128)S(1)}, s32[68]{0:T(128)S(1)}, s32[1]{0:T(128)}, s32[2,64]{1,0:T(2,128)S(1)}) custom-call(s32[64]{0:T(128)S(1)} %copy-done.3, s32[8,64]{1,0:T(8,128)S(1)} %bitcast.3, s32[8,64]{1,0:T(8,128)S(1)} %bitcast.4), custom_call_target="tpu_custom_call" | custom-call | tf_op jit(solution)/shard_map/route/pallas_call | solution.py:245
  7.5 0.0 collective-permute-done.119
  7.6 1.5 %collective-permute-done.118 = bf16[64,512]{1,0:T(8,128)(2,1)S(1)} collective-permute-done((bf16[64,512]{1,0:T(8,128)(2,1)S(1)}, bf16[64,512]{1,0:T(8,128)(2,1)S(1)}, u32[]{:S(2)}, u32[]{:S(2)}) %collective-permute-start.118) | collective-permute-done | bytes 65568 | tf_op jit(solution)/shard_map/ppermute | solution.py:266
  9.0 0.5 %collective-permute-done.117 = bf16[64,512]{1,0:T(8,128)(2,1)S(1)} collective-permute-done((bf16[64,512]{1,0:T(8,128)(2,1)S(1)}, bf16[64,512]{1,0:T(8,128)(2,1)S(1)}, u32[]{:S(2)}, u32[]{:S(2)}) %collective-permute-start.117) | collective-permute-done | bytes 65568 | tf_op jit(solution)/shard_map/ppermute | solution.py:266
  9.5 0.0 copy-start
  9.6 0.1 collective-permute-start.120
  10.3 0.9 %collective-permute-done.120.kv_other = bf16[256,512]{1,0:T(8,128)(2,1)S(1)} collective-permute-done((bf16[256,512]{1,0:T(8,128)(2,1)S(1)}, bf16[256,512]{1,0:T(8,128)(2,1)S(1)}, u32[]{:S(2)}, u32[]{:S(2)}) %collective-permute-start.120) | collective-permute-done | bytes 262176 | tf_op jit(solution)/shard_map/ppermute | solution.py:269
  11.2 0.0 copy-done
  11.2 0.6 %attention.1 = bf16[64,64,128]{2,1,0:T(8,128)(2,1)S(1)} custom-call(s32[17]{0:T(128)S(1)} %get-tuple-element.296.send, s32[2,64]{1,0:T(2,128)S(1)} %get-tuple-element.297.bits, bf16[256,512]{1,0:T(8,128)(2,1)S(1)} %constant_dynamic-update-slice_fusion.kv_own, bf16[256,512]{1,0:T(8,128)(2,1)S(1)} %collective-permute-done.120.kv_other, ...), custom_call_target="tpu_custom_call" | custom-call | tf_op jit(solution)/shard_map/attention/pallas_call | solution.py:271
  11.8 13.0 %conditional.1 = (bf16[64,2048]{1,0:T(8,128)(2,1)}) conditional(s32[]{:T(128)} %bitcast.2, (bf16[64,64,128]{2,1,0:T(8,128)(2,1)S(1)}, s32[68]{0:T(128)S(1)}) %tuple.124, (bf16[64,64,128]{2,1,0:T(8,128)(2,1)S(1)}, s32[68]{0:T(128)S(1)}) %tuple.124, (bf16[64,64,128]{2,1,0:T(8,128)(2,1)S(1)}, ...), branch_computations={%region_0.1_spmd, %region_1.2_spmd, %region_2.3_spmd, %region_3.4_... | conditional | bytes 4718720 | solution.py:281
  11.9 2.7 %collective-permute-start.56 = (bf16[6,64,128]{2,1,0:T(8,128)(2,1)S(1)}, bf16[6,64,128]{2,1,0:T(8,128)(2,1)S(1)}, u32[]{:S(2)}, u32[]{:S(2)}) collective-permute-start(bf16[6,64,128]{2,1,0:T(8,128)(2,1)S(1)} %get-tuple-element.331), channel_id=1, source_target_pairs={{0,2},{1,3},{2,0},{3,1},{4,6},{5,7},{6,4},{7,5},{8,10},{9,11},{10,... | collective-permute-start | bytes 294920 | tf_op jit(solution)/shard_map/cond/branch_15_fun/ppermute | solution.py:219
  14.5 1.3 %collective-permute-start.55 = (bf16[6,64,128]{2,1,0:T(8,128)(2,1)S(1)}, bf16[6,64,128]{2,1,0:T(8,128)(2,1)S(1)}, u32[]{:S(2)}, u32[]{:S(2)}) collective-permute-start(bf16[6,64,128]{2,1,0:T(8,128)(2,1)S(1)} %get-tuple-element.332), channel_id=1, source_target_pairs={{0,3},{1,2},{2,1},{3,0},{4,7},{5,6},{6,5},{7,4},{8,11},{9,10},{10,... | collective-permute-start | bytes 294920 | tf_op jit(solution)/shard_map/cond/branch_15_fun/ppermute | solution.py:219
  15.9 0.2 collective-permute-start.54
  16.1 6.6 %collective-permute-done.56.refs_3_ = bf16[6,64,128]{2,1,0:T(8,128)(2,1)S(1)} collective-permute-done((bf16[6,64,128]{2,1,0:T(8,128)(2,1)S(1)}, bf16[6,64,128]{2,1,0:T(8,128)(2,1)S(1)}, u32[]{:S(2)}, u32[]{:S(2)}) %collective-permute-start.56) | collective-permute-done | bytes 98336 | tf_op jit(solution)/shard_map/cond/branch_15_fun/ppermute | solution.py:219
  22.7 0.0 collective-permute-done.55.refs_2_
  22.7 0.5 %collective-permute-done.54.refs_1_ = bf16[6,64,128]{2,1,0:T(8,128)(2,1)S(1)} collective-permute-done((bf16[6,64,128]{2,1,0:T(8,128)(2,1)S(1)}, bf16[6,64,128]{2,1,0:T(8,128)(2,1)S(1)}, u32[]{:S(2)}, u32[]{:S(2)}) %collective-permute-start.54) | collective-permute-done | bytes 98336 | tf_op jit(solution)/shard_map/cond/branch_15_fun/ppermute | solution.py:219
  23.3 1.3 %place.54 = bf16[64,2048]{1,0:T(8,128)(2,1)} custom-call(s32[68]{0:T(128)S(1)} %get-tuple-element.223.slots, bf16[64,64,128]{2,1,0:T(8,128)(2,1)S(1)} %get-tuple-element.224.refs_0_, bf16[6,64,128]{2,1,0:T(8,128)(2,1)S(1)} %collective-permute-done.54.refs_1_, bf16[6,64,128]{2,1,0:T(8,128)(2,1)S(1)} %collective-permute-done.55.refs_2_, ...), custom_call_target="tpu_custom_call" | custom-call | tf_op jit(solution)/shard_map/cond/branch_15_fun/place/pallas_call | solution.py:224
  (6 shorter events, 0.1 us)
Async XLA Ops:
  0.8 4.6 %copy-start.1 = (s32[64,8]{0,1:T(8,128)S(1)}, s32[64,8]{0,1:T(8,128)}, u32[]{:S(2)}) copy-start(s32[64,8]{0,1:T(8,128)} %param.48) | copy-start | bytes 6148
  0.8 4.6 %copy-start.2 = (s32[64,8]{0,1:T(8,128)S(1)}, s32[64,8]{0,1:T(8,128)}, u32[]{:S(2)}) copy-start(s32[64,8]{0,1:T(8,128)} %param.49) | copy-start | bytes 6148
  0.8 6.8 %collective-permute-start.119 = (bf16[64,512]{1,0:T(8,128)(2,1)S(1)}, bf16[64,512]{1,0:T(8,128)(2,1)S(1)}, u32[]{:S(2)}, u32[]{:S(2)}) collective-permute-start(bf16[64,512]{1,0:T(8,128)(2,1)S(1)} %pad_maximum_fusion), channel_id=1, source_target_pairs={{0,24},{4,28},{8,16},{12,20},{16,8},{20,12},{24,0},{28,4},{1,25},{... | collective-permute-start | bytes 196616 | tf_op jit(solution)/shard_map/ppermute | solution.py:266
  4.8 4.3 %collective-permute-start.118 = (bf16[64,512]{1,0:T(8,128)(2,1)S(1)}, bf16[64,512]{1,0:T(8,128)(2,1)S(1)}, u32[]{:S(2)}, u32[]{:S(2)}) collective-permute-start(bf16[64,512]{1,0:T(8,128)(2,1)S(1)} %pad_maximum_fusion), channel_id=1, source_target_pairs={{0,16},{4,20},{8,24},{12,28},{16,0},{20,4},{24,8},{28,12},{1,17},{... | collective-permute-start | bytes 196616 | tf_op jit(solution)/shard_map/ppermute | solution.py:266
  5.3 4.3 %collective-permute-start.117 = (bf16[64,512]{1,0:T(8,128)(2,1)S(1)}, bf16[64,512]{1,0:T(8,128)(2,1)S(1)}, u32[]{:S(2)}, u32[]{:S(2)}) collective-permute-start(bf16[64,512]{1,0:T(8,128)(2,1)S(1)} %pad_maximum_fusion), channel_id=1, source_target_pairs={{0,8},{4,12},{8,0},{12,4},{16,24},{20,28},{24,16},{28,20},{1,9},{5... | collective-permute-start | bytes 196616 | tf_op jit(solution)/shard_map/ppermute | solution.py:266
  5.4 0.7 %copy-start.3 = (s32[64]{0:T(128)S(1)}, s32[64]{0:T(128)}, u32[]{:S(2)}) copy-start(s32[64]{0:T(128)} %plan.1) | copy-start | bytes 772
  9.5 1.7 %copy-start = (bf16[64,2048]{1,0:T(8,128)(2,1)S(1)}, bf16[64,2048]{1,0:T(8,128)(2,1)}, u32[]{:S(2)}) copy-start(bf16[64,2048]{1,0:T(8,128)(2,1)} %query_ref.1) | copy-start | bytes 786436
  9.6 1.6 %collective-permute-start.120 = (bf16[256,512]{1,0:T(8,128)(2,1)S(1)}, bf16[256,512]{1,0:T(8,128)(2,1)S(1)}, u32[]{:S(2)}, u32[]{:S(2)}) collective-permute-start(bf16[256,512]{1,0:T(8,128)(2,1)S(1)} %constant_dynamic-update-slice_fusion.kv_own), channel_id=1, source_target_pairs={{0,4},{4,0},{8,12},{12,8},{16,20},{20,16},{24,28},{28,24},{1,5},{5... | collective-permute-start | bytes 786440 | tf_op jit(solution)/shard_map/ppermute | solution.py:269
  11.9 10.9 %collective-permute-start.56 = (bf16[6,64,128]{2,1,0:T(8,128)(2,1)S(1)}, bf16[6,64,128]{2,1,0:T(8,128)(2,1)S(1)}, u32[]{:S(2)}, u32[]{:S(2)}) collective-permute-start(bf16[6,64,128]{2,1,0:T(8,128)(2,1)S(1)} %get-tuple-element.331), channel_id=1, source_target_pairs={{0,2},{1,3},{2,0},{3,1},{4,6},{5,7},{6,4},{7,5},{8,10},{9,11},{10,... | collective-permute-start | bytes 294920 | tf_op jit(solution)/shard_map/cond/branch_15_fun/ppermute | solution.py:219
  14.5 8.2 %collective-permute-start.55 = (bf16[6,64,128]{2,1,0:T(8,128)(2,1)S(1)}, bf16[6,64,128]{2,1,0:T(8,128)(2,1)S(1)}, u32[]{:S(2)}, u32[]{:S(2)}) collective-permute-start(bf16[6,64,128]{2,1,0:T(8,128)(2,1)S(1)} %get-tuple-element.332), channel_id=1, source_target_pairs={{0,3},{1,2},{2,1},{3,0},{4,7},{5,6},{6,5},{7,4},{8,11},{9,10},{10,... | collective-permute-start | bytes 294920 | tf_op jit(solution)/shard_map/cond/branch_15_fun/ppermute | solution.py:219
  15.9 7.4 %collective-permute-start.54 = (bf16[6,64,128]{2,1,0:T(8,128)(2,1)S(1)}, bf16[6,64,128]{2,1,0:T(8,128)(2,1)S(1)}, u32[]{:S(2)}, u32[]{:S(2)}) collective-permute-start(bf16[6,64,128]{2,1,0:T(8,128)(2,1)S(1)} %get-tuple-element.333), channel_id=1, source_target_pairs={{0,1},{1,0},{2,3},{3,2},{4,5},{5,4},{6,7},{7,6},{8,9},{9,8},{10,11... | collective-permute-start | bytes 294920 | tf_op jit(solution)/shard_map/cond/branch_15_fun/ppermute | solution.py:219
where the time goes:
time: 25.2 us; the launch traced here: 24.9 us
  waiting for transfers between devices  10 us (40%)
  starting transfers between devices  8.91 us (35%)
  Pallas kernels  3.31 us (13%)
  local copies, waits for them, and re-layouts  1.49 us (6%)
  between operations  0.91 us (4%)
  loops' own time  0.31 us (1%)
    ppermute x3, waiting for transfers between devices, exchange(): lax.ppermute(packed[m * held:m * held + capacities[m]], 'head', [(i, i ^...  7.16 us
    ppermute x3, starting transfers between devices, per_device(): pieces.append(lax.ppermute(kv, 'seq', pairs))  4.6 us
    ppermute x3, starting transfers between devices, exchange(): lax.ppermute(packed[m * held:m * held + capacities[m]], 'head', [(i, i ^...  4.24 us
    ppermute x3, waiting for transfers between devices, per_device(): pieces.append(lax.ppermute(kv, 'seq', pairs))  1.98 us
    pallas_call x1, Pallas kernels, per_device(): pl.pallas_call(functools.partial(route_kernel, head_size, held, levels),...  1.48 us
    pallas_call x1, Pallas kernels, exchange(): pl.pallas_call(functools.partial(place_kernel, head_size, held, [(0, held...  1.25 us
    ppermute x1, waiting for transfers between devices, per_device(): lax.ppermute(kv_own, 'seq', [(i, i ^ 1) for i in range(seq_size)])  0.87 us
    dynamic_slice x1, local copies, waits for them, and re-layouts, per_device(): lax.dynamic_slice_in_dim(rows, kv_at, kv_heads * HD, axis=1)  0.78 us
  transfers between devices with their start and end apart: 7, of which 5 were waited for; matrix products, arithmetic and copies ran while one was open for 0% of the time, Pallas kernels for 6%

commit v1 on v0

--- a/solution.py
+++ b/solution.py
@@ -103,26 +103,37 @@
     send_copy.start()
     own_seq = lax.axis_index("seq")
     rest = (send_copy, bits, kv_own, kv_other, query_ref, out_ref, send_here)
-
-    @pl.when(own_seq < 2)
-    def _():
-        attend(1, held, kv_heads, *rest)
-
-    @pl.when(own_seq >= 2)
-    def _():
-        attend(seq_size // 2, held, kv_heads, *rest)
-
-
-def attend(chips, held, kv_heads, send_copy, bits, kv_own, kv_other, query_ref, out_ref, send_here):
+    chips = seq_size // 2
+
+    def pieces_of(chip):
+        return tuple(m for m in range(chips) if chip ^ m <= chip)
+
+    if chips == 4:
+        cases = [((own_seq >> 1) == chip, pieces_of(chip)) for chip in range(chips)]
+    else:
+        cases = [(own_seq < 2, (0,)), (own_seq >= 2, tuple(range(chips)))]
+    for applies, pieces in cases:
+
+        @pl.when(applies)
+        def _(pieces=pieces):
+            attend(pieces, held, kv_heads, *rest)
+
+
+def attend(pieces, held, kv_heads, send_copy, bits, kv_own, kv_other, query_ref, out_ref, send_here):
     query_len = query_ref.shape[0]
     key_len = query_len
     own_seq = lax.axis_index("seq")
     own_head = lax.axis_index("head")
-    half = chips * key_len
-
-    piece = lax.broadcasted_iota(jnp.int32, (1, 2 * half), 1) // key_len
-    core = jnp.where(piece < chips, own_seq & 1, 1 - (own_seq & 1))
-    block = ((own_seq >> 1) ^ (piece & (chips - 1))) * 2 + core
+    keys = 2 * len(pieces) * key_len
+
+    place = lax.broadcasted_iota(jnp.int32, (1, keys), 1) // key_len
+    own_core = place < len(pieces)
+    place = jnp.where(own_core, place, place - len(pieces))
+    piece = jnp.zeros_like(place)
+    for at, m in enumerate(pieces):
+        piece = jnp.where(place == at, m, piece)
+    core = jnp.where(own_core, own_seq & 1, 1 - (own_seq & 1))
+    block = ((own_seq >> 1) ^ piece) * 2 + core
     back = own_seq - block
     present = back >= 0
     back_shift = jnp.maximum(back, 0)
@@ -139,10 +150,25 @@
     score_scale = HD ** (-0.5) * math.log2(math.e)
     per_kv = held // kv_heads
 
+    def rows_of(at):
+        runs = []
+        for m in pieces:
+            if runs and runs[-1][1] == m:
+                runs[-1][1] = m + 1
+            else:
+                runs.append([m, m + 1])
+        return jnp.concatenate(
+            [
+                ref[first * key_len : last * key_len, at : at + HD]
+                for ref in (kv_own, kv_other)
+                for first, last in runs
+            ],
+            axis=0,
+        )
+
     def scores_of(lead):
         heads = range(lead, min(lead + HEADS_AT_ONCE, held))
-        key_at = lead // per_kv * HD
-        key = jnp.concatenate([ref[:half, key_at : key_at + HD] for ref in (kv_own, kv_other)], axis=0)
+        key = rows_of(lead // per_kv * HD)
         query = jnp.concatenate([query_ref[:, i * HD : (i + 1) * HD] for i in heads], axis=0)
         return lax.dot_general(
             query, key, (((1,), (1,)), ((), ())), preferred_element_type=jnp.float32
@@ -155,14 +181,13 @@
         scores = following
         if lead + HEADS_AT_ONCE < held:
             following = scores_of(lead + HEADS_AT_ONCE)
-        value_at = (lead // per_kv + kv_heads) * HD
-        value = jnp.concatenate([ref[:half, value_at : value_at + HD] for ref in (kv_own, kv_other)], axis=0)
+        value = rows_of((lead // per_kv + kv_heads) * HD)
         weights = []
         totals = []
         for at, i in enumerate(heads):
             masked = scores[at * query_len : (at + 1) * query_len] + bias[i : i + 1, :]
             own_block = jnp.where(causal, masked[:, :LANES], floor_value)
-            masked = own_block if 2 * half == LANES else jnp.concatenate([own_block, masked[:, LANES:]], axis=1)
+            masked = own_block if keys == LANES else jnp.concatenate([own_block, masked[:, LANES:]], axis=1)
             row_max = jnp.max(masked, axis=1, keepdims=True)
             weight = jnp.exp2((masked - row_max) * score_scale)
             totals.append(1.0 / jnp.sum(weight, axis=1, keepdims=True))
@@ -173,8 +198,8 @@
         for at, i in enumerate(heads):
             mix = mixture[at * query_len : (at + 1) * query_len]
             ready.append((i, (mix * totals[at]).astype(out_ref.dtype)))
-        if chips > 1 or lead + HEADS_AT_ONCE >= held:
-            if chips == 1 or lead == 0:
+        if len(pieces) > 1 or lead + HEADS_AT_ONCE >= held:
+            if len(pieces) == 1 or lead == 0:
                 send_copy.wait()
             for i, rows in ready:
                 out_ref[send_here[i]] = rows

time: 25.2 us -> 24.4 us (0.968)
  waiting for transfers between devices: 10 us -> 8.96 us
    ppermute x3, waiting for transfers between devices: 7.16 us -> 6.11 us  [exchange(): lax.ppermute(packed[m * held:m * held + capacities[m]], 'head', [(i, i ^...]
where the time goes in v1:
time: 24.4 us; the launch traced here: 23.9 us
  waiting for transfers between devices  8.96 us (37%)
  starting transfers between devices  8.91 us (37%)
  Pallas kernels  3.32 us (14%)
  local copies, waits for them, and re-layouts  1.48 us (6%)
  between operations  0.91 us (4%)
  loops' own time  0.31 us (1%)
    ppermute x3, waiting for transfers between devices, exchange(): lax.ppermute(packed[m * held:m * held + capacities[m]], 'head', [(i, i ^...  6.11 us
    ppermute x3, starting transfers between devices, per_device(): pieces.append(lax.ppermute(kv, 'seq', pairs))  4.6 us
    ppermute x3, starting transfers between devices, exchange(): lax.ppermute(packed[m * held:m * held + capacities[m]], 'head', [(i, i ^...  4.24 us
    ppermute x3, waiting for transfers between devices, per_device(): pieces.append(lax.ppermute(kv, 'seq', pairs))  1.98 us
    pallas_call x1, Pallas kernels, per_device(): pl.pallas_call(functools.partial(route_kernel, head_size, held, levels),...  1.48 us
    pallas_call x1, Pallas kernels, exchange(): pl.pallas_call(functools.partial(place_kernel, head_size, held, [(0, held...  1.26 us
    ppermute x1, waiting for transfers between devices, per_device(): lax.ppermute(kv_own, 'seq', [(i, i ^ 1) for i in range(seq_size)])  0.87 us
    dynamic_slice x1, local copies, waits for them, and re-layouts, per_device(): lax.dynamic_slice_in_dim(rows, kv_at, kv_heads * HD, axis=1)  0.78 us
  transfers between devices with their start and end apart: 7, of which 5 were waited for; matrix products, arithmetic and copies ran while one was open for 0% of the time, Pallas kernels for 6%

profile of v1, /device:TPU:0, one launch (start us, length us, event | category | flops | bytes accessed | tf_op | source)
XLA Modules:
  0.0 23.9 jit_solution(9585479153013403903)
XLA Ops:
  0.0 0.8 %constant_dynamic-slice_fusion = (bf16[64,256]{1,0:T(8,128)(2,1)S(1)}, bf16[64,256]{1,0:T(8,128)(2,1)S(1)}) fusion(bf16[64,1024]{1,0:T(8,128)(2,1)} %param.47, s32[]{:T(128)S(6)} %select_n.10, bf16[64,1024]{1,0:T(8,128)(2,1)} %param.46), kind=kLoop, calls=%fused_computation.5 | loop fusion | bytes 131076 | tf_op jit(solution)/shard_map/dynamic_slice | solution.py:286
  0.8 0.0 copy-start.1
  0.8 0.0 copy-start.2
  0.8 4.0 %collective-permute-start.119 = (bf16[64,512]{1,0:T(8,128)(2,1)S(1)}, bf16[64,512]{1,0:T(8,128)(2,1)S(1)}, u32[]{:S(2)}, u32[]{:S(2)}) collective-permute-start(bf16[64,512]{1,0:T(8,128)(2,1)S(1)} %pad_maximum_fusion), channel_id=1, source_target_pairs={{0,24},{4,28},{8,16},{12,20},{16,8},{20,12},{24,0},{28,4},{1,25},{... | collective-permute-start | bytes 196616 | tf_op jit(solution)/shard_map/ppermute | solution.py:291
  4.8 0.5 %collective-permute-start.118 = (bf16[64,512]{1,0:T(8,128)(2,1)S(1)}, bf16[64,512]{1,0:T(8,128)(2,1)S(1)}, u32[]{:S(2)}, u32[]{:S(2)}) collective-permute-start(bf16[64,512]{1,0:T(8,128)(2,1)S(1)} %pad_maximum_fusion), channel_id=1, source_target_pairs={{0,16},{4,20},{8,24},{12,28},{16,0},{20,4},{24,8},{28,12},{1,17},{... | collective-permute-start | bytes 196616 | tf_op jit(solution)/shard_map/ppermute | solution.py:291
  5.3 0.1 collective-permute-start.117
  5.4 0.0 copy-start.3
  5.4 0.0 copy-done.1
  5.4 0.0 copy-done.2
  5.4 0.6 %copy-done.3 = s32[64]{0:T(128)S(1)} copy-done((s32[64]{0:T(128)S(1)}, s32[64]{0:T(128)}, u32[]{:S(2)}) %copy-start.3) | copy-done | bytes 280
  6.1 1.5 %route.1 = (s32[17]{0:T(128)S(1)}, s32[68]{0:T(128)S(1)}, s32[1]{0:T(128)}, s32[2,64]{1,0:T(2,128)S(1)}) custom-call(s32[64]{0:T(128)S(1)} %copy-done.3, s32[8,64]{1,0:T(8,128)S(1)} %bitcast.3, s32[8,64]{1,0:T(8,128)S(1)} %bitcast.4), custom_call_target="tpu_custom_call" | custom-call | tf_op jit(solution)/shard_map/route/pallas_call | solution.py:270
  7.5 0.0 collective-permute-done.119
  7.6 1.5 %collective-permute-done.118 = bf16[64,512]{1,0:T(8,128)(2,1)S(1)} collective-permute-done((bf16[64,512]{1,0:T(8,128)(2,1)S(1)}, bf16[64,512]{1,0:T(8,128)(2,1)S(1)}, u32[]{:S(2)}, u32[]{:S(2)}) %collective-permute-start.118) | collective-permute-done | bytes 65568 | tf_op jit(solution)/shard_map/ppermute | solution.py:291
  9.0 0.5 %collective-permute-done.117 = bf16[64,512]{1,0:T(8,128)(2,1)S(1)} collective-permute-done((bf16[64,512]{1,0:T(8,128)(2,1)S(1)}, bf16[64,512]{1,0:T(8,128)(2,1)S(1)}, u32[]{:S(2)}, u32[]{:S(2)}) %collective-permute-start.117) | collective-permute-done | bytes 65568 | tf_op jit(solution)/shard_map/ppermute | solution.py:291
  9.5 0.0 copy-start
  9.6 0.1 collective-permute-start.120
  10.3 0.9 %collective-permute-done.120.kv_other = bf16[256,512]{1,0:T(8,128)(2,1)S(1)} collective-permute-done((bf16[256,512]{1,0:T(8,128)(2,1)S(1)}, bf16[256,512]{1,0:T(8,128)(2,1)S(1)}, u32[]{:S(2)}, u32[]{:S(2)}) %collective-permute-start.120) | collective-permute-done | bytes 262176 | tf_op jit(solution)/shard_map/ppermute | solution.py:294
  11.2 0.0 copy-done
  11.2 0.6 %attention.1 = bf16[64,64,128]{2,1,0:T(8,128)(2,1)S(1)} custom-call(s32[17]{0:T(128)S(1)} %get-tuple-element.296.send, s32[2,64]{1,0:T(2,128)S(1)} %get-tuple-element.297.bits, bf16[256,512]{1,0:T(8,128)(2,1)S(1)} %constant_dynamic-update-slice_fusion.kv_own, bf16[256,512]{1,0:T(8,128)(2,1)S(1)} %collective-permute-done.120.kv_other, ...), custom_call_target="tpu_custom_call" | custom-call | tf_op jit(solution)/shard_map/attention/pallas_call | solution.py:296
  11.8 11.9 %conditional.1 = (bf16[64,2048]{1,0:T(8,128)(2,1)}) conditional(s32[]{:T(128)} %bitcast.2, (bf16[64,64,128]{2,1,0:T(8,128)(2,1)S(1)}, s32[68]{0:T(128)S(1)}) %tuple.124, (bf16[64,64,128]{2,1,0:T(8,128)(2,1)S(1)}, s32[68]{0:T(128)S(1)}) %tuple.124, (bf16[64,64,128]{2,1,0:T(8,128)(2,1)S(1)}, ...), branch_computations={%region_0.1_spmd, %region_1.2_spmd, %region_2.3_spmd, %region_3.4_... | conditional | bytes 4718720 | solution.py:306
  11.9 2.7 %collective-permute-start.26 = (bf16[5,64,128]{2,1,0:T(8,128)(2,1)S(1)}, bf16[5,64,128]{2,1,0:T(8,128)(2,1)S(1)}, u32[]{:S(2)}, u32[]{:S(2)}) collective-permute-start(bf16[5,64,128]{2,1,0:T(8,128)(2,1)S(1)} %get-tuple-element.310), channel_id=1, source_target_pairs={{0,2},{1,3},{2,0},{3,1},{4,6},{5,7},{6,4},{7,5},{8,10},{9,11},{10,... | collective-permute-start | bytes 245768 | tf_op jit(solution)/shard_map/cond/branch_3_fun/ppermute | solution.py:244
  14.5 1.3 %collective-permute-start.25 = (bf16[5,64,128]{2,1,0:T(8,128)(2,1)S(1)}, bf16[5,64,128]{2,1,0:T(8,128)(2,1)S(1)}, u32[]{:S(2)}, u32[]{:S(2)}) collective-permute-start(bf16[5,64,128]{2,1,0:T(8,128)(2,1)S(1)} %get-tuple-element.311), channel_id=1, source_target_pairs={{0,3},{1,2},{2,1},{3,0},{4,7},{5,6},{6,5},{7,4},{8,11},{9,10},{10,... | collective-permute-start | bytes 245768 | tf_op jit(solution)/shard_map/cond/branch_3_fun/ppermute | solution.py:244
  15.9 0.2 collective-permute-start.24
  16.1 5.4 %collective-permute-done.26.refs_3_ = bf16[5,64,128]{2,1,0:T(8,128)(2,1)S(1)} collective-permute-done((bf16[5,64,128]{2,1,0:T(8,128)(2,1)S(1)}, bf16[5,64,128]{2,1,0:T(8,128)(2,1)S(1)}, u32[]{:S(2)}, u32[]{:S(2)}) %collective-permute-start.26) | collective-permute-done | bytes 81952 | tf_op jit(solution)/shard_map/cond/branch_3_fun/ppermute | solution.py:244
  21.5 0.0 collective-permute-done.25.refs_2_
  21.5 0.7 %collective-permute-done.24.refs_1_ = bf16[5,64,128]{2,1,0:T(8,128)(2,1)S(1)} collective-permute-done((bf16[5,64,128]{2,1,0:T(8,128)(2,1)S(1)}, bf16[5,64,128]{2,1,0:T(8,128)(2,1)S(1)}, u32[]{:S(2)}, u32[]{:S(2)}) %collective-permute-start.24) | collective-permute-done | bytes 81952 | tf_op jit(solution)/shard_map/cond/branch_3_fun/ppermute | solution.py:244
  22.2 1.3 %place.42 = bf16[64,2048]{1,0:T(8,128)(2,1)} custom-call(s32[68]{0:T(128)S(1)} %get-tuple-element.175.slots, bf16[64,64,128]{2,1,0:T(8,128)(2,1)S(1)} %get-tuple-element.176.refs_0_, bf16[5,64,128]{2,1,0:T(8,128)(2,1)S(1)} %collective-permute-done.24.refs_1_, bf16[5,64,128]{2,1,0:T(8,128)(2,1)S(1)} %collective-permute-done.25.refs_2_, ...), custom_call_target="tpu_custom_call" | custom-call | tf_op jit(solution)/shard_map/cond/branch_3_fun/place/pallas_call | solution.py:249
  (6 shorter events, 0.1 us)
Async XLA Ops:
  0.8 4.6 %copy-start.1 = (s32[64,8]{0,1:T(8,128)S(1)}, s32[64,8]{0,1:T(8,128)}, u32[]{:S(2)}) copy-start(s32[64,8]{0,1:T(8,128)} %param.48) | copy-start | bytes 6148
  0.8 4.6 %copy-start.2 = (s32[64,8]{0,1:T(8,128)S(1)}, s32[64,8]{0,1:T(8,128)}, u32[]{:S(2)}) copy-start(s32[64,8]{0,1:T(8,128)} %param.49) | copy-start | bytes 6148
  0.8 6.8 %collective-permute-start.119 = (bf16[64,512]{1,0:T(8,128)(2,1)S(1)}, bf16[64,512]{1,0:T(8,128)(2,1)S(1)}, u32[]{:S(2)}, u32[]{:S(2)}) collective-permute-start(bf16[64,512]{1,0:T(8,128)(2,1)S(1)} %pad_maximum_fusion), channel_id=1, source_target_pairs={{0,24},{4,28},{8,16},{12,20},{16,8},{20,12},{24,0},{28,4},{1,25},{... | collective-permute-start | bytes 196616 | tf_op jit(solution)/shard_map/ppermute | solution.py:291
  4.8 4.3 %collective-permute-start.118 = (bf16[64,512]{1,0:T(8,128)(2,1)S(1)}, bf16[64,512]{1,0:T(8,128)(2,1)S(1)}, u32[]{:S(2)}, u32[]{:S(2)}) collective-permute-start(bf16[64,512]{1,0:T(8,128)(2,1)S(1)} %pad_maximum_fusion), channel_id=1, source_target_pairs={{0,16},{4,20},{8,24},{12,28},{16,0},{20,4},{24,8},{28,12},{1,17},{... | collective-permute-start | bytes 196616 | tf_op jit(solution)/shard_map/ppermute | solution.py:291
  5.3 4.3 %collective-permute-start.117 = (bf16[64,512]{1,0:T(8,128)(2,1)S(1)}, bf16[64,512]{1,0:T(8,128)(2,1)S(1)}, u32[]{:S(2)}, u32[]{:S(2)}) collective-permute-start(bf16[64,512]{1,0:T(8,128)(2,1)S(1)} %pad_maximum_fusion), channel_id=1, source_target_pairs={{0,8},{4,12},{8,0},{12,4},{16,24},{20,28},{24,16},{28,20},{1,9},{5... | collective-permute-start | bytes 196616 | tf_op jit(solution)/shard_map/ppermute | solution.py:291
  5.4 0.7 %copy-start.3 = (s32[64]{0:T(128)S(1)}, s32[64]{0:T(128)}, u32[]{:S(2)}) copy-start(s32[64]{0:T(128)} %plan.1) | copy-start | bytes 772
  9.5 1.7 %copy-start = (bf16[64,2048]{1,0:T(8,128)(2,1)S(1)}, bf16[64,2048]{1,0:T(8,128)(2,1)}, u32[]{:S(2)}) copy-start(bf16[64,2048]{1,0:T(8,128)(2,1)} %query_ref.1) | copy-start | bytes 786436
  9.6 1.6 %collective-permute-start.120 = (bf16[256,512]{1,0:T(8,128)(2,1)S(1)}, bf16[256,512]{1,0:T(8,128)(2,1)S(1)}, u32[]{:S(2)}, u32[]{:S(2)}) collective-permute-start(bf16[256,512]{1,0:T(8,128)(2,1)S(1)} %constant_dynamic-update-slice_fusion.kv_own), channel_id=1, source_target_pairs={{0,4},{4,0},{8,12},{12,8},{16,20},{20,16},{24,28},{28,24},{1,5},{5... | collective-permute-start | bytes 786440 | tf_op jit(solution)/shard_map/ppermute | solution.py:294
  11.9 9.6 %collective-permute-start.26 = (bf16[5,64,128]{2,1,0:T(8,128)(2,1)S(1)}, bf16[5,64,128]{2,1,0:T(8,128)(2,1)S(1)}, u32[]{:S(2)}, u32[]{:S(2)}) collective-permute-start(bf16[5,64,128]{2,1,0:T(8,128)(2,1)S(1)} %get-tuple-element.310), channel_id=1, source_target_pairs={{0,2},{1,3},{2,0},{3,1},{4,6},{5,7},{6,4},{7,5},{8,10},{9,11},{10,... | collective-permute-start | bytes 245768 | tf_op jit(solution)/shard_map/cond/branch_3_fun/ppermute | solution.py:244
  14.5 7.0 %collective-permute-start.25 = (bf16[5,64,128]{2,1,0:T(8,128)(2,1)S(1)}, bf16[5,64,128]{2,1,0:T(8,128)(2,1)S(1)}, u32[]{:S(2)}, u32[]{:S(2)}) collective-permute-start(bf16[5,64,128]{2,1,0:T(8,128)(2,1)S(1)} %get-tuple-element.311), channel_id=1, source_target_pairs={{0,3},{1,2},{2,1},{3,0},{4,7},{5,6},{6,5},{7,4},{8,11},{9,10},{10,... | collective-permute-start | bytes 245768 | tf_op jit(solution)/shard_map/cond/branch_3_fun/ppermute | solution.py:244
  15.9 6.3 %collective-permute-start.24 = (bf16[5,64,128]{2,1,0:T(8,128)(2,1)S(1)}, bf16[5,64,128]{2,1,0:T(8,128)(2,1)S(1)}, u32[]{:S(2)}, u32[]{:S(2)}) collective-permute-start(bf16[5,64,128]{2,1,0:T(8,128)(2,1)S(1)} %get-tuple-element.312), channel_id=1, source_target_pairs={{0,1},{1,0},{2,3},{3,2},{4,5},{5,4},{6,7},{7,6},{8,9},{9,8},{10,11... | collective-permute-start | bytes 245768 | tf_op jit(solution)/shard_map/cond/branch_3_fun/ppermute | solution.py:244

commit v2 on v1

--- a/solution.py
+++ b/solution.py
@@ -221,10 +221,10 @@
 
 
 SHAPES = (
-    (4, 5, 4), (7, 4, 4), (4, 6, 4), (5, 5, 5), (8, 5, 4), (4, 4, 6), (4, 7, 4), (5, 6, 5), (6, 4, 6), (6, 6, 4),
-    (8, 5, 5), (9, 6, 4), (4, 4, 7), (5, 5, 6), (5, 7, 5), (6, 6, 6), (7, 4, 7), (8, 7, 4), (9, 6, 5), (5, 5, 7),
-    (5, 8, 5), (6, 7, 6), (7, 5, 7), (8, 4, 8), (9, 7, 5), (11, 6, 6), (6, 6, 7), (5, 9, 5), (6, 8, 6), (7, 7, 7),
-    (8, 5, 8), (6, 6, 8), (7, 8, 7), (6, 6, 9), (8, 8, 8), (7, 10, 7), (9, 9, 9), (11, 10, 10),
+    (4, 4, 4), (5, 5, 4), (8, 4, 4), (5, 5, 5), (6, 6, 4), (9, 5, 4), (5, 6, 5), (6, 6, 5), (7, 7, 4), (5, 4, 6),
+    (7, 5, 5), (9, 5, 5), (5, 7, 5), (6, 6, 6), (7, 7, 5), (8, 8, 4), (6, 4, 7), (8, 4, 6), (7, 7, 6), (8, 8, 5),
+    (6, 5, 7), (7, 4, 8), (11, 6, 6), (7, 7, 7), (8, 8, 6), (9, 9, 5), (7, 5, 8), (8, 4, 9), (8, 8, 7), (9, 10, 5),
+    (7, 6, 8), (8, 5, 9), (8, 8, 8), (9, 9, 7), (6, 6, 9), (9, 6, 10), (9, 9, 9), (11, 8, 10),
 )
 
 
@@ -239,7 +239,7 @@
 
 
 def exchange(head_size, held, capacities, packed, slots):
-    order = sorted(range(1, head_size), key=lambda m: (m >= head_size // 2, -m))
+    order = sorted(range(1, head_size), key=lambda m: (m == head_size // 2, -m))
     arrived = [
         lax.ppermute(
             packed[m * held : m * held + capacities[m]], "head", [(i, i ^ m) for i in range(head_size)]

time: 24.4 us -> 24.2 us (level); the launches traced: 23.9 us -> 24 us
  transfers between devices with their start and end apart: 7 -> 7, of which waited for: 5 -> 4; matrix products, arithmetic and copies ran while one was open for 0% -> 0% of each run, Pallas kernels for 6% -> 6%
where the time goes in v2:
time: 24.2 us; the launch traced here: 24 us
  starting transfers between devices  9.12 us (38%)
  waiting for transfers between devices  8.88 us (37%)
  Pallas kernels  3.32 us (14%)
  local copies, waits for them, and re-layouts  1.49 us (6%)
  between operations  0.91 us (4%)
  loops' own time  0.31 us (1%)
    ppermute x3, waiting for transfers between devices, exchange(): lax.ppermute(packed[m * held:m * held + capacities[m]], 'head', [(i, i ^...  6.02 us
    ppermute x3, starting transfers between devices, per_device(): pieces.append(lax.ppermute(kv, 'seq', pairs))  4.6 us
    ppermute x3, starting transfers between devices, exchange(): lax.ppermute(packed[m * held:m * held + capacities[m]], 'head', [(i, i ^...  4.45 us
    ppermute x3, waiting for transfers between devices, per_device(): pieces.append(lax.ppermute(kv, 'seq', pairs))  1.98 us
    pallas_call x1, Pallas kernels, per_device(): pl.pallas_call(functools.partial(route_kernel, head_size, held, levels),...  1.47 us
    pallas_call x1, Pallas kernels, exchange(): pl.pallas_call(functools.partial(place_kernel, head_size, held, [(0, held...  1.26 us
    ppermute x1, waiting for transfers between devices, per_device(): lax.ppermute(kv_own, 'seq', [(i, i ^ 1) for i in range(seq_size)])  0.87 us
    dynamic_slice x1, local copies, waits for them, and re-layouts, per_device(): lax.dynamic_slice_in_dim(rows, kv_at, kv_heads * HD, axis=1)  0.78 us
  transfers between devices with their start and end apart: 7, of which 4 were waited for; matrix products, arithmetic and copies ran while one was open for 0% of the time, Pallas kernels for 6%

profile of v2, /device:TPU:0, one launch (start us, length us, event | category | flops | bytes accessed | tf_op | source)
XLA Modules:
  0.0 24.0 jit_solution(12698735018145969233)
XLA Ops:
  0.0 0.8 %constant_dynamic-slice_fusion = (bf16[64,256]{1,0:T(8,128)(2,1)S(1)}, bf16[64,256]{1,0:T(8,128)(2,1)S(1)}) fusion(bf16[64,1024]{1,0:T(8,128)(2,1)} %param.47, s32[]{:T(128)S(6)} %select_n.10, bf16[64,1024]{1,0:T(8,128)(2,1)} %param.46), kind=kLoop, calls=%fused_computation.5 | loop fusion | bytes 131076 | tf_op jit(solution)/shard_map/dynamic_slice | solution.py:286
  0.8 0.0 copy-start.1
  0.8 0.0 copy-start.2
  0.8 4.0 %collective-permute-start.119 = (bf16[64,512]{1,0:T(8,128)(2,1)S(1)}, bf16[64,512]{1,0:T(8,128)(2,1)S(1)}, u32[]{:S(2)}, u32[]{:S(2)}) collective-permute-start(bf16[64,512]{1,0:T(8,128)(2,1)S(1)} %pad_maximum_fusion), channel_id=1, source_target_pairs={{0,24},{4,28},{8,16},{12,20},{16,8},{20,12},{24,0},{28,4},{1,25},{... | collective-permute-start | bytes 196616 | tf_op jit(solution)/shard_map/ppermute | solution.py:291
  4.8 0.5 %collective-permute-start.118 = (bf16[64,512]{1,0:T(8,128)(2,1)S(1)}, bf16[64,512]{1,0:T(8,128)(2,1)S(1)}, u32[]{:S(2)}, u32[]{:S(2)}) collective-permute-start(bf16[64,512]{1,0:T(8,128)(2,1)S(1)} %pad_maximum_fusion), channel_id=1, source_target_pairs={{0,16},{4,20},{8,24},{12,28},{16,0},{20,4},{24,8},{28,12},{1,17},{... | collective-permute-start | bytes 196616 | tf_op jit(solution)/shard_map/ppermute | solution.py:291
  5.3 0.1 collective-permute-start.117
  5.4 0.0 copy-start.3
  5.4 0.0 copy-done.1
  5.4 0.0 copy-done.2
  5.4 0.6 %copy-done.3 = s32[64]{0:T(128)S(1)} copy-done((s32[64]{0:T(128)S(1)}, s32[64]{0:T(128)}, u32[]{:S(2)}) %copy-start.3) | copy-done | bytes 280
  6.1 1.5 %route.1 = (s32[17]{0:T(128)S(1)}, s32[68]{0:T(128)S(1)}, s32[1]{0:T(128)}, s32[2,64]{1,0:T(2,128)S(1)}) custom-call(s32[64]{0:T(128)S(1)} %copy-done.3, s32[8,64]{1,0:T(8,128)S(1)} %bitcast.3, s32[8,64]{1,0:T(8,128)S(1)} %bitcast.4), custom_call_target="tpu_custom_call" | custom-call | tf_op jit(solution)/shard_map/route/pallas_call | solution.py:270
  7.5 0.0 collective-permute-done.119
  7.6 1.5 %collective-permute-done.118 = bf16[64,512]{1,0:T(8,128)(2,1)S(1)} collective-permute-done((bf16[64,512]{1,0:T(8,128)(2,1)S(1)}, bf16[64,512]{1,0:T(8,128)(2,1)S(1)}, u32[]{:S(2)}, u32[]{:S(2)}) %collective-permute-start.118) | collective-permute-done | bytes 65568 | tf_op jit(solution)/shard_map/ppermute | solution.py:291
  9.0 0.5 %collective-permute-done.117 = bf16[64,512]{1,0:T(8,128)(2,1)S(1)} collective-permute-done((bf16[64,512]{1,0:T(8,128)(2,1)S(1)}, bf16[64,512]{1,0:T(8,128)(2,1)S(1)}, u32[]{:S(2)}, u32[]{:S(2)}) %collective-permute-start.117) | collective-permute-done | bytes 65568 | tf_op jit(solution)/shard_map/ppermute | solution.py:291
  9.5 0.0 copy-start
  9.6 0.1 collective-permute-start.120
  10.3 0.9 %collective-permute-done.120.kv_other = bf16[256,512]{1,0:T(8,128)(2,1)S(1)} collective-permute-done((bf16[256,512]{1,0:T(8,128)(2,1)S(1)}, bf16[256,512]{1,0:T(8,128)(2,1)S(1)}, u32[]{:S(2)}, u32[]{:S(2)}) %collective-permute-start.120) | collective-permute-done | bytes 262176 | tf_op jit(solution)/shard_map/ppermute | solution.py:294
  11.2 0.0 copy-done
  11.2 0.6 %attention.1 = bf16[64,64,128]{2,1,0:T(8,128)(2,1)S(1)} custom-call(s32[17]{0:T(128)S(1)} %get-tuple-element.296.send, s32[2,64]{1,0:T(2,128)S(1)} %get-tuple-element.297.bits, bf16[256,512]{1,0:T(8,128)(2,1)S(1)} %constant_dynamic-update-slice_fusion.kv_own, bf16[256,512]{1,0:T(8,128)(2,1)S(1)} %collective-permute-done.120.kv_other, ...), custom_call_target="tpu_custom_call" | custom-call | tf_op jit(solution)/shard_map/attention/pallas_call | solution.py:296
  11.8 12.1 %conditional.1 = (bf16[64,2048]{1,0:T(8,128)(2,1)}) conditional(s32[]{:T(128)} %bitcast.2, (bf16[64,64,128]{2,1,0:T(8,128)(2,1)S(1)}, s32[68]{0:T(128)S(1)}) %tuple.124, (bf16[64,64,128]{2,1,0:T(8,128)(2,1)S(1)}, s32[68]{0:T(128)S(1)}) %tuple.124, (bf16[64,64,128]{2,1,0:T(8,128)(2,1)S(1)}, ...), branch_computations={%region_0.1_spmd, %region_1.2_spmd, %region_2.3_spmd, %region_3.4_... | conditional | bytes 4718720 | solution.py:306
  11.8 2.7 %collective-permute-start.53 = (bf16[6,64,128]{2,1,0:T(8,128)(2,1)S(1)}, bf16[6,64,128]{2,1,0:T(8,128)(2,1)S(1)}, u32[]{:S(2)}, u32[]{:S(2)}) collective-permute-start(bf16[6,64,128]{2,1,0:T(8,128)(2,1)S(1)} %get-tuple-element.314), channel_id=1, source_target_pairs={{0,2},{1,3},{2,0},{3,1},{4,6},{5,7},{6,4},{7,5},{8,10},{9,11},{10,... | collective-permute-start | bytes 294920 | tf_op jit(solution)/shard_map/cond/branch_4_fun/ppermute | solution.py:244
  14.5 1.6 %collective-permute-start.52 = (bf16[6,64,128]{2,1,0:T(8,128)(2,1)S(1)}, bf16[6,64,128]{2,1,0:T(8,128)(2,1)S(1)}, u32[]{:S(2)}, u32[]{:S(2)}) collective-permute-start(bf16[6,64,128]{2,1,0:T(8,128)(2,1)S(1)} %get-tuple-element.315), channel_id=1, source_target_pairs={{0,1},{1,0},{2,3},{3,2},{4,5},{5,4},{6,7},{7,6},{8,9},{9,8},{10,11... | collective-permute-start | bytes 294920 | tf_op jit(solution)/shard_map/cond/branch_4_fun/ppermute | solution.py:244
  16.1 0.2 collective-permute-start.51
  16.3 6.0 %collective-permute-done.51.refs_1_ = bf16[4,64,128]{2,1,0:T(8,128)(2,1)S(1)} collective-permute-done((bf16[4,64,128]{2,1,0:T(8,128)(2,1)S(1)}, bf16[4,64,128]{2,1,0:T(8,128)(2,1)S(1)}, u32[]{:S(2)}, u32[]{:S(2)}) %collective-permute-start.51) | collective-permute-done | bytes 65568 | tf_op jit(solution)/shard_map/cond/branch_4_fun/ppermute | solution.py:244
  22.3 0.0 collective-permute-done.53.refs_3_
  22.3 0.0 collective-permute-done.52.refs_2_
  22.3 1.3 %place.43 = bf16[64,2048]{1,0:T(8,128)(2,1)} custom-call(s32[68]{0:T(128)S(1)} %get-tuple-element.180.slots, bf16[64,64,128]{2,1,0:T(8,128)(2,1)S(1)} %get-tuple-element.181.refs_0_, bf16[4,64,128]{2,1,0:T(8,128)(2,1)S(1)} %collective-permute-done.51.refs_1_, bf16[6,64,128]{2,1,0:T(8,128)(2,1)S(1)} %collective-permute-done.52.refs_2_, ...), custom_call_target="tpu_custom_call" | custom-call | tf_op jit(solution)/shard_map/cond/branch_4_fun/place/pallas_call | solution.py:249
  (7 shorter events, 0.1 us)
Async XLA Ops:
  0.8 4.6 %copy-start.1 = (s32[64,8]{0,1:T(8,128)S(1)}, s32[64,8]{0,1:T(8,128)}, u32[]{:S(2)}) copy-start(s32[64,8]{0,1:T(8,128)} %param.48) | copy-start | bytes 6148
  0.8 4.6 %copy-start.2 = (s32[64,8]{0,1:T(8,128)S(1)}, s32[64,8]{0,1:T(8,128)}, u32[]{:S(2)}) copy-start(s32[64,8]{0,1:T(8,128)} %param.49) | copy-start | bytes 6148
  0.8 6.7 %collective-permute-start.119 = (bf16[64,512]{1,0:T(8,128)(2,1)S(1)}, bf16[64,512]{1,0:T(8,128)(2,1)S(1)}, u32[]{:S(2)}, u32[]{:S(2)}) collective-permute-start(bf16[64,512]{1,0:T(8,128)(2,1)S(1)} %pad_maximum_fusion), channel_id=1, source_target_pairs={{0,24},{4,28},{8,16},{12,20},{16,8},{20,12},{24,0},{28,4},{1,25},{... | collective-permute-start | bytes 196616 | tf_op jit(solution)/shard_map/ppermute | solution.py:291
  4.8 4.3 %collective-permute-start.118 = (bf16[64,512]{1,0:T(8,128)(2,1)S(1)}, bf16[64,512]{1,0:T(8,128)(2,1)S(1)}, u32[]{:S(2)}, u32[]{:S(2)}) collective-permute-start(bf16[64,512]{1,0:T(8,128)(2,1)S(1)} %pad_maximum_fusion), channel_id=1, source_target_pairs={{0,16},{4,20},{8,24},{12,28},{16,0},{20,4},{24,8},{28,12},{1,17},{... | collective-permute-start | bytes 196616 | tf_op jit(solution)/shard_map/ppermute | solution.py:291
  5.3 4.3 %collective-permute-start.117 = (bf16[64,512]{1,0:T(8,128)(2,1)S(1)}, bf16[64,512]{1,0:T(8,128)(2,1)S(1)}, u32[]{:S(2)}, u32[]{:S(2)}) collective-permute-start(bf16[64,512]{1,0:T(8,128)(2,1)S(1)} %pad_maximum_fusion), channel_id=1, source_target_pairs={{0,8},{4,12},{8,0},{12,4},{16,24},{20,28},{24,16},{28,20},{1,9},{5... | collective-permute-start | bytes 196616 | tf_op jit(solution)/shard_map/ppermute | solution.py:291
  5.4 0.7 %copy-start.3 = (s32[64]{0:T(128)S(1)}, s32[64]{0:T(128)}, u32[]{:S(2)}) copy-start(s32[64]{0:T(128)} %plan.1) | copy-start | bytes 772
  9.5 1.7 %copy-start = (bf16[64,2048]{1,0:T(8,128)(2,1)S(1)}, bf16[64,2048]{1,0:T(8,128)(2,1)}, u32[]{:S(2)}) copy-start(bf16[64,2048]{1,0:T(8,128)(2,1)} %query_ref.1) | copy-start | bytes 786436
  9.6 1.6 %collective-permute-start.120 = (bf16[256,512]{1,0:T(8,128)(2,1)S(1)}, bf16[256,512]{1,0:T(8,128)(2,1)S(1)}, u32[]{:S(2)}, u32[]{:S(2)}) collective-permute-start(bf16[256,512]{1,0:T(8,128)(2,1)S(1)} %constant_dynamic-update-slice_fusion.kv_own), channel_id=1, source_target_pairs={{0,4},{4,0},{8,12},{12,8},{16,20},{20,16},{24,28},{28,24},{1,5},{5... | collective-permute-start | bytes 786440 | tf_op jit(solution)/shard_map/ppermute | solution.py:294
  11.8 10.5 %collective-permute-start.53 = (bf16[6,64,128]{2,1,0:T(8,128)(2,1)S(1)}, bf16[6,64,128]{2,1,0:T(8,128)(2,1)S(1)}, u32[]{:S(2)}, u32[]{:S(2)}) collective-permute-start(bf16[6,64,128]{2,1,0:T(8,128)(2,1)S(1)} %get-tuple-element.314), channel_id=1, source_target_pairs={{0,2},{1,3},{2,0},{3,1},{4,6},{5,7},{6,4},{7,5},{8,10},{9,11},{10,... | collective-permute-start | bytes 294920 | tf_op jit(solution)/shard_map/cond/branch_4_fun/ppermute | solution.py:244
  14.5 7.8 %collective-permute-start.52 = (bf16[6,64,128]{2,1,0:T(8,128)(2,1)S(1)}, bf16[6,64,128]{2,1,0:T(8,128)(2,1)S(1)}, u32[]{:S(2)}, u32[]{:S(2)}) collective-permute-start(bf16[6,64,128]{2,1,0:T(8,128)(2,1)S(1)} %get-tuple-element.315), channel_id=1, source_target_pairs={{0,1},{1,0},{2,3},{3,2},{4,5},{5,4},{6,7},{7,6},{8,9},{9,8},{10,11... | collective-permute-start | bytes 294920 | tf_op jit(solution)/shard_map/cond/branch_4_fun/ppermute | solution.py:244
  16.1 6.2 %collective-permute-start.51 = (bf16[4,64,128]{2,1,0:T(8,128)(2,1)S(1)}, bf16[4,64,128]{2,1,0:T(8,128)(2,1)S(1)}, u32[]{:S(2)}, u32[]{:S(2)}) collective-permute-start(bf16[4,64,128]{2,1,0:T(8,128)(2,1)S(1)} %slice.246), channel_id=1, source_target_pairs={{0,3},{1,2},{2,1},{3,0},{4,7},{5,6},{6,5},{7,4},{8,11},{9,10},{10,... | collective-permute-start | bytes 196616 | tf_op jit(solution)/shard_map/cond/branch_4_fun/ppermute | solution.py:244
